TPU v7x, 512 devices: a whole 4x8x8 slice. The times are simulated.
512 devices in a mesh: chain: 64 (over y, z_lo, x), tp: 8 (over z_hi, core).
Axes of the slice: x: 4, y: 8, z: 8 (z_hi: 4, z_lo: 2; z = z_hi * 2 + z_lo), core: 2. Of those that a mesh axis runs over, the one named last changes fastest.
Arguments:
- hidden: bfloat16 [8192, 5120], P('chain', 'tp'), may hold values from -1000 to 1000
- segments: int32 [8192], P('chain'), may hold values from 0 to 255, never falling along the last dimension, each value on 1 to 128 neighbouring positions
- in_gain: float32 [5120], replicated, may hold values from 0.1 to 1.9
- q_gain: float32 [128], replicated, may hold values from 0.5 to 2.5
- k_gain: float32 [128], replicated, may hold values from 0.5 to 2.5
- w_query: bfloat16 [5120, 4096], P('chain', 'tp'), may hold values from -0.078125 to 0.078125
- w_key: bfloat16 [5120, 1024], P('chain', 'tp'), may hold values from -0.078125 to 0.078125
- w_value: bfloat16 [5120, 1024], P('chain', 'tp'), may hold values from -0.078125 to 0.078125
Outputs:
- context: bfloat16 [8192, 4096], P('chain', 'tp')
Inputs may be any that keep to these rules, and one draw needn't show every extreme that they name: `segments`: document ids never fall along the tokens; a document holds at most 128 tokens and some document holds exactly 128.
All inputs are finite; a program needn't handle non-finite values.
Results may differ from a plain program's by a relative error of at most 0.0085.
Values may be sent and summed in bfloat16 or wider, within the bound.
A program may use at most 64 MiB of HBM per device.

v0:
```python
import jax
import jax.numpy as jnp
from jax import lax
from jax.sharding import PartitionSpec as P

D = 5120
HEAD = 128


EPSILON = 1e-06
ROPE_BASE = 1000000.0


def passed_along(x, axis, by):
    count = lax.axis_size(axis)
    return lax.ppermute(x, axis, [(i, (i + by) % count) for i in range(count)])


def root_norm(values, gain):
    return values * lax.rsqrt(jnp.mean(values * values, axis=-1, keepdims=True) + EPSILON) * gain


def positions(segment_ids):
    length = segment_ids.shape[0]
    ordinal = jnp.arange(length, dtype=jnp.int32)
    change = jnp.concatenate(
        [jnp.ones((1,), jnp.int32), (segment_ids[1:] != segment_ids[:-1]).astype(jnp.int32)]
    )
    starts = lax.cummax(ordinal * change, axis=0)
    return (ordinal - starts, ordinal)


def rotate(values, offsets):
    half_dim = values.shape[-1] // 2
    ladder = jnp.arange(half_dim, dtype=jnp.float32)
    frequency = ROPE_BASE ** (-2.0 * ladder / values.shape[-1])
    angles = offsets.astype(jnp.float32)[:, None] * frequency[None, :]
    cosine = jnp.cos(angles)[:, None, :]
    sine = jnp.sin(angles)[:, None, :]
    first = values[..., :half_dim]
    second = values[..., half_dim:]
    return jnp.concatenate(
        [first * cosine - second * sine, second * cosine + first * sine], axis=-1
    )


def attention(queries, key_rows, value_rows, segment_ids, ordinal):
    length, group, head_dim = queries.shape
    block = min(256, length)
    scale = head_dim ** (-0.5)

    def one_block(start):
        rows = queries
        rows = jnp.transpose(rows, (1, 0, 2)).reshape(group * block, head_dim)
        logits = jnp.dot(rows, key_rows.T, preferred_element_type=jnp.float32) * scale
        allowed = (ordinal[None, :] <= ordinal[:, None]) & (
            segment_ids[None, :] == segment_ids[:, None]
        )
        allowed = jnp.tile(allowed, (group, 1))
        expo = jnp.where(allowed, jnp.exp(logits), 0.0)
        attend_weights = (expo / jnp.sum(expo, axis=-1, keepdims=True)).astype(jnp.bfloat16)
        context = jnp.dot(attend_weights, value_rows, preferred_element_type=jnp.float32).astype(
            jnp.bfloat16
        )
        return jnp.transpose(context.reshape(group, block, head_dim), (1, 0, 2))

    starts = jnp.arange(length // block, dtype=jnp.int32) * block
    blocks = lax.map(one_block, starts)
    return blocks.reshape(length, group, head_dim)


def pass_on(pieces):
    return passed_along((pieces[0], pieces[1], pieces[2]), "chain", 1)


def deposit(buffers, pieces, source):
    return tuple(
        (
            lax.dynamic_update_index_in_dim(store, piece, source, 0)
            for store, piece in zip(buffers, pieces)
        )
    )


def per_device(hidden, segments, in_gain, q_gain, k_gain, w_query, w_key, w_value):
    pieces = (w_query, w_key, w_value)
    chain_size = lax.axis_size("chain")
    my_index = lax.axis_index("chain")
    buffers = tuple((jnp.zeros((chain_size,) + piece.shape, piece.dtype) for piece in pieces))
    buffers = deposit(buffers, pieces, my_index)

    def forward_section(section, state):
        stores, carried = state
        carried = pass_on(carried)
        stores = deposit(stores, carried, (my_index - section) % chain_size)
        return (stores, carried)

    buffers, pieces = lax.fori_loop(1, chain_size, forward_section, (buffers, pieces))
    full_query, full_key, full_value = tuple(
        (store.reshape(chain_size * store.shape[1], store.shape[2]) for store in buffers)
    )
    local_float = hidden.astype(jnp.float32)
    squares_local = jnp.sum(local_float * local_float, axis=1)
    squares_total = lax.psum(squares_local, "tp")
    inverse = lax.rsqrt(squares_total / D + EPSILON)
    length = hidden.shape[0]
    matrices = (full_query, full_key, full_value)
    normed_part = (
        lax.all_gather(hidden, "tp", axis=1, tiled=True).astype(jnp.float32)
        * inverse[:, None]
        * in_gain[None, :]
    ).astype(jnp.bfloat16)
    query_full, key_part, value_part = tuple(
        (jnp.dot(normed_part, matrix, preferred_element_type=jnp.float32) for matrix in matrices)
    )
    query_cols = full_query.shape[1]
    key_cols = full_key.shape[1]
    local_query = query_cols // HEAD
    local_kv = key_cols // HEAD
    offsets, ordinal = positions(segments)
    queries = query_full.reshape(length, local_query, HEAD)
    key_rows = key_part.reshape(length, local_kv, HEAD)
    value_rows = value_part.astype(jnp.bfloat16).reshape(length, local_kv, HEAD)
    queries = rotate(root_norm(queries, q_gain), offsets).astype(jnp.bfloat16)
    key_rows = rotate(root_norm(key_rows, k_gain), offsets).astype(jnp.bfloat16)

    def one_head(kv_head):
        key_one = lax.dynamic_index_in_dim(key_rows, kv_head, 1, keepdims=False)
        value_one = lax.dynamic_index_in_dim(value_rows, kv_head, 1, keepdims=False)
        return attention(queries, key_one, value_one, segments, ordinal)

    heads = lax.map(one_head, jnp.arange(local_kv, dtype=jnp.int32))
    return jnp.transpose(heads, (1, 0, 2, 3)).reshape(length, local_query * HEAD)


def solution(mesh):
    placed = (
        P("chain", "tp"),
        P("chain"),
        P(),
        P(),
        P(),
        P("chain", "tp"),
        P("chain", "tp"),
        P("chain", "tp"),
    )
    return jax.shard_map(
        per_device, mesh=mesh, in_specs=placed, out_specs=P("chain", "tp"), check_vma=False
    )
```

profile of v0, /device:TPU:1, one launch (start us, length us, event | category | flops | bytes accessed | tf_op | source)
XLA Modules:
  0.0 972.6 jit_solution(15513668236827800494)
XLA Ops:
  13.2 843.8 %while.21 = (s32[]{:T(128)}, bf16[64,80,512]{2,1,0:T(8,128)(2,1)}, bf16[64,80,128]{2,1,0:T(8,128)(2,1)S(1)}, bf16[64,80,128]{2,1,0:T(8,128)(2,1)S(1)}, bf16[80,5...) while((s32[]{:T(128)}, bf16[64,80,512]{2,1,0:T(8,128)(2,1)}, ...), condition=%wide.region_3.4_spmd, body=%wide.region_2.3_spmd.sunk | while | flops 17 | bytes 983444 | solution.py:98
  13.2 3.9 collective-permute-start.1
  24.3 4.7 collective-permute-done.2
  38.4 3.9 collective-permute-done.2
  51.8 3.8 collective-permute-done.2
  65.0 3.8 collective-permute-done.2
  78.3 3.8 collective-permute-done.2
  91.6 3.8 collective-permute-done.2
  104.9 3.8 collective-permute-done.2
  131.4 3.8 collective-permute-done.2
  145.1 3.8 collective-permute-done.2
  158.4 3.8 collective-permute-done.2
  171.7 4.2 collective-permute-done.2
  185.3 3.8 collective-permute-done.2
  198.6 3.8 collective-permute-done.2
  211.8 3.8 collective-permute-done.2
  225.1 3.8 collective-permute-done.2
  238.4 3.8 collective-permute-done.2
  251.7 3.8 collective-permute-done.2
  265.0 3.8 collective-permute-done.2
  278.3 3.8 collective-permute-done.2
  304.8 3.8 collective-permute-done.2
  318.6 3.8 collective-permute-done.2
  331.8 3.8 collective-permute-done.2
  345.1 4.2 collective-permute-done.2
  358.7 3.8 collective-permute-done.2
  372.0 4.1 collective-permute-done.2
  385.6 3.8 collective-permute-done.2
  398.9 3.8 collective-permute-done.2
  412.1 3.8 collective-permute-done.2
  425.4 3.8 collective-permute-done.2
  492.3 3.8 collective-permute-done.2
  518.9 4.3 collective-permute-done.2
  532.6 3.8 collective-permute-done.2
  545.9 4.3 collective-permute-done.2
  559.7 3.8 collective-permute-done.2
  599.5 3.8 collective-permute-done.2
  626.1 3.8 collective-permute-done.2
  679.2 3.8 collective-permute-done.2
  692.5 4.4 collective-permute-done.2
  706.3 3.8 collective-permute-done.2
  719.6 3.9 collective-permute-done.2
  746.2 3.8 collective-permute-done.2
  759.4 3.8 collective-permute-done.2
  786.0 3.8 collective-permute-done.2
  857.0 7.9 copy.12
  865.0 90.9 %psum.7 = f32[128]{0:T(128)S(1)} all-reduce(f32[128]{0:T(128)S(1)} %multiply_reduce_fusion), channel_id=1, replica_groups=mesh['chain'=64,'tp'=8] {'tp'}, use_global_device_ids=true, to_apply=%region_1.2 | all-reduce | flops 128 | bytes 1024 | tf_op jit(solution)/shard_map/psum | solution.py:104
  958.8 4.1 multiply_reduce_fusion.1
  (764 shorter events, 678.6 us)
Async XLA Ops:
  6.5 949.7 %all-gather.2.cloned.1.call-start = ((), (), s32[]{:S(2)}) async-start(), calls=%async_computation | async-start | bytes 1474560 | tf_op jit(solution)/shard_map/all_gather | solution.py:109
  13.2 11.1 %collective-permute-start.1 = (bf16[80,128]{1,0:T(8,128)(2,1)S(1)}, bf16[80,128]{1,0:T(8,128)(2,1)S(1)}, u32[]{:S(2)}, u32[]{:S(2)}) collective-permute-start(bf16[80,128]{1,0:T(8,128)(2,1)S(1)} %get-tuple-element.352), channel_id=1, source_target_pairs={{0,8},{8,16},{16,24},{24,32},{32,40},{40,48},{48,56},{56,64},{64,7... | collective-permute-start | bytes 61448 | tf_op jit(solution)/shard_map/while/body/eval_jaxpr/ppermute | solution.py:16
  17.1 11.9 %collective-permute-start = (bf16[80,512]{1,0:T(8,128)(2,1)S(1)}, bf16[80,512]{1,0:T(8,128)(2,1)S(1)}, u32[]{:S(2)}, u32[]{:S(2)}) collective-permute-start(bf16[80,512]{1,0:T(8,128)(2,1)S(1)} %get-tuple-element.351), channel_id=1, source_target_pairs={{0,8},{8,16},{16,24},{24,32},{32,40},{40,48},{48,56},{56,64},{64,7... | collective-permute-start | bytes 245768 | tf_op jit(solution)/shard_map/while/body/eval_jaxpr/ppermute | solution.py:16
  31.6 10.8 %collective-permute-start = (bf16[80,512]{1,0:T(8,128)(2,1)S(1)}, bf16[80,512]{1,0:T(8,128)(2,1)S(1)}, u32[]{:S(2)}, u32[]{:S(2)}) collective-permute-start(bf16[80,512]{1,0:T(8,128)(2,1)S(1)} %get-tuple-element.351), channel_id=1, source_target_pairs={{0,8},{8,16},{16,24},{24,32},{32,40},{40,48},{48,56},{56,64},{64,7... | collective-permute-start | bytes 245768 | tf_op jit(solution)/shard_map/while/body/eval_jaxpr/ppermute | solution.py:16
  44.9 10.7 %collective-permute-start = (bf16[80,512]{1,0:T(8,128)(2,1)S(1)}, bf16[80,512]{1,0:T(8,128)(2,1)S(1)}, u32[]{:S(2)}, u32[]{:S(2)}) collective-permute-start(bf16[80,512]{1,0:T(8,128)(2,1)S(1)} %get-tuple-element.351), channel_id=1, source_target_pairs={{0,8},{8,16},{16,24},{24,32},{32,40},{40,48},{48,56},{56,64},{64,7... | collective-permute-start | bytes 245768 | tf_op jit(solution)/shard_map/while/body/eval_jaxpr/ppermute | solution.py:16
  58.2 10.7 %collective-permute-start = (bf16[80,512]{1,0:T(8,128)(2,1)S(1)}, bf16[80,512]{1,0:T(8,128)(2,1)S(1)}, u32[]{:S(2)}, u32[]{:S(2)}) collective-permute-start(bf16[80,512]{1,0:T(8,128)(2,1)S(1)} %get-tuple-element.351), channel_id=1, source_target_pairs={{0,8},{8,16},{16,24},{24,32},{32,40},{40,48},{48,56},{56,64},{64,7... | collective-permute-start | bytes 245768 | tf_op jit(solution)/shard_map/while/body/eval_jaxpr/ppermute | solution.py:16
  71.5 10.7 %collective-permute-start = (bf16[80,512]{1,0:T(8,128)(2,1)S(1)}, bf16[80,512]{1,0:T(8,128)(2,1)S(1)}, u32[]{:S(2)}, u32[]{:S(2)}) collective-permute-start(bf16[80,512]{1,0:T(8,128)(2,1)S(1)} %get-tuple-element.351), channel_id=1, source_target_pairs={{0,8},{8,16},{16,24},{24,32},{32,40},{40,48},{48,56},{56,64},{64,7... | collective-permute-start | bytes 245768 | tf_op jit(solution)/shard_map/while/body/eval_jaxpr/ppermute | solution.py:16
  84.8 10.7 %collective-permute-start = (bf16[80,512]{1,0:T(8,128)(2,1)S(1)}, bf16[80,512]{1,0:T(8,128)(2,1)S(1)}, u32[]{:S(2)}, u32[]{:S(2)}) collective-permute-start(bf16[80,512]{1,0:T(8,128)(2,1)S(1)} %get-tuple-element.351), channel_id=1, source_target_pairs={{0,8},{8,16},{16,24},{24,32},{32,40},{40,48},{48,56},{56,64},{64,7... | collective-permute-start | bytes 245768 | tf_op jit(solution)/shard_map/while/body/eval_jaxpr/ppermute | solution.py:16
  98.0 10.7 %collective-permute-start = (bf16[80,512]{1,0:T(8,128)(2,1)S(1)}, bf16[80,512]{1,0:T(8,128)(2,1)S(1)}, u32[]{:S(2)}, u32[]{:S(2)}) collective-permute-start(bf16[80,512]{1,0:T(8,128)(2,1)S(1)} %get-tuple-element.351), channel_id=1, source_target_pairs={{0,8},{8,16},{16,24},{24,32},{32,40},{40,48},{48,56},{56,64},{64,7... | collective-permute-start | bytes 245768 | tf_op jit(solution)/shard_map/while/body/eval_jaxpr/ppermute | solution.py:16
  111.3 10.7 %collective-permute-start = (bf16[80,512]{1,0:T(8,128)(2,1)S(1)}, bf16[80,512]{1,0:T(8,128)(2,1)S(1)}, u32[]{:S(2)}, u32[]{:S(2)}) collective-permute-start(bf16[80,512]{1,0:T(8,128)(2,1)S(1)} %get-tuple-element.351), channel_id=1, source_target_pairs={{0,8},{8,16},{16,24},{24,32},{32,40},{40,48},{48,56},{56,64},{64,7... | collective-permute-start | bytes 245768 | tf_op jit(solution)/shard_map/while/body/eval_jaxpr/ppermute | solution.py:16
  124.6 10.7 %collective-permute-start = (bf16[80,512]{1,0:T(8,128)(2,1)S(1)}, bf16[80,512]{1,0:T(8,128)(2,1)S(1)}, u32[]{:S(2)}, u32[]{:S(2)}) collective-permute-start(bf16[80,512]{1,0:T(8,128)(2,1)S(1)} %get-tuple-element.351), channel_id=1, source_target_pairs={{0,8},{8,16},{16,24},{24,32},{32,40},{40,48},{48,56},{56,64},{64,7... | collective-permute-start | bytes 245768 | tf_op jit(solution)/shard_map/while/body/eval_jaxpr/ppermute | solution.py:16
  137.9 11.1 %collective-permute-start = (bf16[80,512]{1,0:T(8,128)(2,1)S(1)}, bf16[80,512]{1,0:T(8,128)(2,1)S(1)}, u32[]{:S(2)}, u32[]{:S(2)}) collective-permute-start(bf16[80,512]{1,0:T(8,128)(2,1)S(1)} %get-tuple-element.351), channel_id=1, source_target_pairs={{0,8},{8,16},{16,24},{24,32},{32,40},{40,48},{48,56},{56,64},{64,7... | collective-permute-start | bytes 245768 | tf_op jit(solution)/shard_map/while/body/eval_jaxpr/ppermute | solution.py:16
  151.6 10.7 %collective-permute-start = (bf16[80,512]{1,0:T(8,128)(2,1)S(1)}, bf16[80,512]{1,0:T(8,128)(2,1)S(1)}, u32[]{:S(2)}, u32[]{:S(2)}) collective-permute-start(bf16[80,512]{1,0:T(8,128)(2,1)S(1)} %get-tuple-element.351), channel_id=1, source_target_pairs={{0,8},{8,16},{16,24},{24,32},{32,40},{40,48},{48,56},{56,64},{64,7... | collective-permute-start | bytes 245768 | tf_op jit(solution)/shard_map/while/body/eval_jaxpr/ppermute | solution.py:16
  164.9 11.0 %collective-permute-start = (bf16[80,512]{1,0:T(8,128)(2,1)S(1)}, bf16[80,512]{1,0:T(8,128)(2,1)S(1)}, u32[]{:S(2)}, u32[]{:S(2)}) collective-permute-start(bf16[80,512]{1,0:T(8,128)(2,1)S(1)} %get-tuple-element.351), channel_id=1, source_target_pairs={{0,8},{8,16},{16,24},{24,32},{32,40},{40,48},{48,56},{56,64},{64,7... | collective-permute-start | bytes 245768 | tf_op jit(solution)/shard_map/while/body/eval_jaxpr/ppermute | solution.py:16
  178.5 10.7 %collective-permute-start = (bf16[80,512]{1,0:T(8,128)(2,1)S(1)}, bf16[80,512]{1,0:T(8,128)(2,1)S(1)}, u32[]{:S(2)}, u32[]{:S(2)}) collective-permute-start(bf16[80,512]{1,0:T(8,128)(2,1)S(1)} %get-tuple-element.351), channel_id=1, source_target_pairs={{0,8},{8,16},{16,24},{24,32},{32,40},{40,48},{48,56},{56,64},{64,7... | collective-permute-start | bytes 245768 | tf_op jit(solution)/shard_map/while/body/eval_jaxpr/ppermute | solution.py:16
  191.7 10.7 %collective-permute-start = (bf16[80,512]{1,0:T(8,128)(2,1)S(1)}, bf16[80,512]{1,0:T(8,128)(2,1)S(1)}, u32[]{:S(2)}, u32[]{:S(2)}) collective-permute-start(bf16[80,512]{1,0:T(8,128)(2,1)S(1)} %get-tuple-element.351), channel_id=1, source_target_pairs={{0,8},{8,16},{16,24},{24,32},{32,40},{40,48},{48,56},{56,64},{64,7... | collective-permute-start | bytes 245768 | tf_op jit(solution)/shard_map/while/body/eval_jaxpr/ppermute | solution.py:16
  205.0 10.7 %collective-permute-start = (bf16[80,512]{1,0:T(8,128)(2,1)S(1)}, bf16[80,512]{1,0:T(8,128)(2,1)S(1)}, u32[]{:S(2)}, u32[]{:S(2)}) collective-permute-start(bf16[80,512]{1,0:T(8,128)(2,1)S(1)} %get-tuple-element.351), channel_id=1, source_target_pairs={{0,8},{8,16},{16,24},{24,32},{32,40},{40,48},{48,56},{56,64},{64,7... | collective-permute-start | bytes 245768 | tf_op jit(solution)/shard_map/while/body/eval_jaxpr/ppermute | solution.py:16
  218.3 10.7 %collective-permute-start = (bf16[80,512]{1,0:T(8,128)(2,1)S(1)}, bf16[80,512]{1,0:T(8,128)(2,1)S(1)}, u32[]{:S(2)}, u32[]{:S(2)}) collective-permute-start(bf16[80,512]{1,0:T(8,128)(2,1)S(1)} %get-tuple-element.351), channel_id=1, source_target_pairs={{0,8},{8,16},{16,24},{24,32},{32,40},{40,48},{48,56},{56,64},{64,7... | collective-permute-start | bytes 245768 | tf_op jit(solution)/shard_map/while/body/eval_jaxpr/ppermute | solution.py:16
  231.6 10.7 %collective-permute-start = (bf16[80,512]{1,0:T(8,128)(2,1)S(1)}, bf16[80,512]{1,0:T(8,128)(2,1)S(1)}, u32[]{:S(2)}, u32[]{:S(2)}) collective-permute-start(bf16[80,512]{1,0:T(8,128)(2,1)S(1)} %get-tuple-element.351), channel_id=1, source_target_pairs={{0,8},{8,16},{16,24},{24,32},{32,40},{40,48},{48,56},{56,64},{64,7... | collective-permute-start | bytes 245768 | tf_op jit(solution)/shard_map/while/body/eval_jaxpr/ppermute | solution.py:16
  244.9 10.7 %collective-permute-start = (bf16[80,512]{1,0:T(8,128)(2,1)S(1)}, bf16[80,512]{1,0:T(8,128)(2,1)S(1)}, u32[]{:S(2)}, u32[]{:S(2)}) collective-permute-start(bf16[80,512]{1,0:T(8,128)(2,1)S(1)} %get-tuple-element.351), channel_id=1, source_target_pairs={{0,8},{8,16},{16,24},{24,32},{32,40},{40,48},{48,56},{56,64},{64,7... | collective-permute-start | bytes 245768 | tf_op jit(solution)/shard_map/while/body/eval_jaxpr/ppermute | solution.py:16
  258.2 10.7 %collective-permute-start = (bf16[80,512]{1,0:T(8,128)(2,1)S(1)}, bf16[80,512]{1,0:T(8,128)(2,1)S(1)}, u32[]{:S(2)}, u32[]{:S(2)}) collective-permute-start(bf16[80,512]{1,0:T(8,128)(2,1)S(1)} %get-tuple-element.351), channel_id=1, source_target_pairs={{0,8},{8,16},{16,24},{24,32},{32,40},{40,48},{48,56},{56,64},{64,7... | collective-permute-start | bytes 245768 | tf_op jit(solution)/shard_map/while/body/eval_jaxpr/ppermute | solution.py:16
  271.4 10.7 %collective-permute-start = (bf16[80,512]{1,0:T(8,128)(2,1)S(1)}, bf16[80,512]{1,0:T(8,128)(2,1)S(1)}, u32[]{:S(2)}, u32[]{:S(2)}) collective-permute-start(bf16[80,512]{1,0:T(8,128)(2,1)S(1)} %get-tuple-element.351), channel_id=1, source_target_pairs={{0,8},{8,16},{16,24},{24,32},{32,40},{40,48},{48,56},{56,64},{64,7... | collective-permute-start | bytes 245768 | tf_op jit(solution)/shard_map/while/body/eval_jaxpr/ppermute | solution.py:16
  284.7 10.7 %collective-permute-start = (bf16[80,512]{1,0:T(8,128)(2,1)S(1)}, bf16[80,512]{1,0:T(8,128)(2,1)S(1)}, u32[]{:S(2)}, u32[]{:S(2)}) collective-permute-start(bf16[80,512]{1,0:T(8,128)(2,1)S(1)} %get-tuple-element.351), channel_id=1, source_target_pairs={{0,8},{8,16},{16,24},{24,32},{32,40},{40,48},{48,56},{56,64},{64,7... | collective-permute-start | bytes 245768 | tf_op jit(solution)/shard_map/while/body/eval_jaxpr/ppermute | solution.py:16
  298.0 10.7 %collective-permute-start = (bf16[80,512]{1,0:T(8,128)(2,1)S(1)}, bf16[80,512]{1,0:T(8,128)(2,1)S(1)}, u32[]{:S(2)}, u32[]{:S(2)}) collective-permute-start(bf16[80,512]{1,0:T(8,128)(2,1)S(1)} %get-tuple-element.351), channel_id=1, source_target_pairs={{0,8},{8,16},{16,24},{24,32},{32,40},{40,48},{48,56},{56,64},{64,7... | collective-permute-start | bytes 245768 | tf_op jit(solution)/shard_map/while/body/eval_jaxpr/ppermute | solution.py:16
  311.3 11.1 %collective-permute-start = (bf16[80,512]{1,0:T(8,128)(2,1)S(1)}, bf16[80,512]{1,0:T(8,128)(2,1)S(1)}, u32[]{:S(2)}, u32[]{:S(2)}) collective-permute-start(bf16[80,512]{1,0:T(8,128)(2,1)S(1)} %get-tuple-element.351), channel_id=1, source_target_pairs={{0,8},{8,16},{16,24},{24,32},{32,40},{40,48},{48,56},{56,64},{64,7... | collective-permute-start | bytes 245768 | tf_op jit(solution)/shard_map/while/body/eval_jaxpr/ppermute | solution.py:16
  325.0 10.7 %collective-permute-start = (bf16[80,512]{1,0:T(8,128)(2,1)S(1)}, bf16[80,512]{1,0:T(8,128)(2,1)S(1)}, u32[]{:S(2)}, u32[]{:S(2)}) collective-permute-start(bf16[80,512]{1,0:T(8,128)(2,1)S(1)} %get-tuple-element.351), channel_id=1, source_target_pairs={{0,8},{8,16},{16,24},{24,32},{32,40},{40,48},{48,56},{56,64},{64,7... | collective-permute-start | bytes 245768 | tf_op jit(solution)/shard_map/while/body/eval_jaxpr/ppermute | solution.py:16
  338.3 11.0 %collective-permute-start = (bf16[80,512]{1,0:T(8,128)(2,1)S(1)}, bf16[80,512]{1,0:T(8,128)(2,1)S(1)}, u32[]{:S(2)}, u32[]{:S(2)}) collective-permute-start(bf16[80,512]{1,0:T(8,128)(2,1)S(1)} %get-tuple-element.351), channel_id=1, source_target_pairs={{0,8},{8,16},{16,24},{24,32},{32,40},{40,48},{48,56},{56,64},{64,7... | collective-permute-start | bytes 245768 | tf_op jit(solution)/shard_map/while/body/eval_jaxpr/ppermute | solution.py:16
  351.9 10.7 %collective-permute-start = (bf16[80,512]{1,0:T(8,128)(2,1)S(1)}, bf16[80,512]{1,0:T(8,128)(2,1)S(1)}, u32[]{:S(2)}, u32[]{:S(2)}) collective-permute-start(bf16[80,512]{1,0:T(8,128)(2,1)S(1)} %get-tuple-element.351), channel_id=1, source_target_pairs={{0,8},{8,16},{16,24},{24,32},{32,40},{40,48},{48,56},{56,64},{64,7... | collective-permute-start | bytes 245768 | tf_op jit(solution)/shard_map/while/body/eval_jaxpr/ppermute | solution.py:16
  365.2 11.0 %collective-permute-start = (bf16[80,512]{1,0:T(8,128)(2,1)S(1)}, bf16[80,512]{1,0:T(8,128)(2,1)S(1)}, u32[]{:S(2)}, u32[]{:S(2)}) collective-permute-start(bf16[80,512]{1,0:T(8,128)(2,1)S(1)} %get-tuple-element.351), channel_id=1, source_target_pairs={{0,8},{8,16},{16,24},{24,32},{32,40},{40,48},{48,56},{56,64},{64,7... | collective-permute-start | bytes 245768 | tf_op jit(solution)/shard_map/while/body/eval_jaxpr/ppermute | solution.py:16
  378.8 10.7 %collective-permute-start = (bf16[80,512]{1,0:T(8,128)(2,1)S(1)}, bf16[80,512]{1,0:T(8,128)(2,1)S(1)}, u32[]{:S(2)}, u32[]{:S(2)}) collective-permute-start(bf16[80,512]{1,0:T(8,128)(2,1)S(1)} %get-tuple-element.351), channel_id=1, source_target_pairs={{0,8},{8,16},{16,24},{24,32},{32,40},{40,48},{48,56},{56,64},{64,7... | collective-permute-start | bytes 245768 | tf_op jit(solution)/shard_map/while/body/eval_jaxpr/ppermute | solution.py:16
  392.0 10.7 %collective-permute-start = (bf16[80,512]{1,0:T(8,128)(2,1)S(1)}, bf16[80,512]{1,0:T(8,128)(2,1)S(1)}, u32[]{:S(2)}, u32[]{:S(2)}) collective-permute-start(bf16[80,512]{1,0:T(8,128)(2,1)S(1)} %get-tuple-element.351), channel_id=1, source_target_pairs={{0,8},{8,16},{16,24},{24,32},{32,40},{40,48},{48,56},{56,64},{64,7... | collective-permute-start | bytes 245768 | tf_op jit(solution)/shard_map/while/body/eval_jaxpr/ppermute | solution.py:16
  405.3 10.7 %collective-permute-start = (bf16[80,512]{1,0:T(8,128)(2,1)S(1)}, bf16[80,512]{1,0:T(8,128)(2,1)S(1)}, u32[]{:S(2)}, u32[]{:S(2)}) collective-permute-start(bf16[80,512]{1,0:T(8,128)(2,1)S(1)} %get-tuple-element.351), channel_id=1, source_target_pairs={{0,8},{8,16},{16,24},{24,32},{32,40},{40,48},{48,56},{56,64},{64,7... | collective-permute-start | bytes 245768 | tf_op jit(solution)/shard_map/while/body/eval_jaxpr/ppermute | solution.py:16
  418.6 10.7 %collective-permute-start = (bf16[80,512]{1,0:T(8,128)(2,1)S(1)}, bf16[80,512]{1,0:T(8,128)(2,1)S(1)}, u32[]{:S(2)}, u32[]{:S(2)}) collective-permute-start(bf16[80,512]{1,0:T(8,128)(2,1)S(1)} %get-tuple-element.351), channel_id=1, source_target_pairs={{0,8},{8,16},{16,24},{24,32},{32,40},{40,48},{48,56},{56,64},{64,7... | collective-permute-start | bytes 245768 | tf_op jit(solution)/shard_map/while/body/eval_jaxpr/ppermute | solution.py:16
  431.9 10.7 %collective-permute-start = (bf16[80,512]{1,0:T(8,128)(2,1)S(1)}, bf16[80,512]{1,0:T(8,128)(2,1)S(1)}, u32[]{:S(2)}, u32[]{:S(2)}) collective-permute-start(bf16[80,512]{1,0:T(8,128)(2,1)S(1)} %get-tuple-element.351), channel_id=1, source_target_pairs={{0,8},{8,16},{16,24},{24,32},{32,40},{40,48},{48,56},{56,64},{64,7... | collective-permute-start | bytes 245768 | tf_op jit(solution)/shard_map/while/body/eval_jaxpr/ppermute | solution.py:16
  445.2 10.7 %collective-permute-start = (bf16[80,512]{1,0:T(8,128)(2,1)S(1)}, bf16[80,512]{1,0:T(8,128)(2,1)S(1)}, u32[]{:S(2)}, u32[]{:S(2)}) collective-permute-start(bf16[80,512]{1,0:T(8,128)(2,1)S(1)} %get-tuple-element.351), channel_id=1, source_target_pairs={{0,8},{8,16},{16,24},{24,32},{32,40},{40,48},{48,56},{56,64},{64,7... | collective-permute-start | bytes 245768 | tf_op jit(solution)/shard_map/while/body/eval_jaxpr/ppermute | solution.py:16
  458.5 10.7 %collective-permute-start = (bf16[80,512]{1,0:T(8,128)(2,1)S(1)}, bf16[80,512]{1,0:T(8,128)(2,1)S(1)}, u32[]{:S(2)}, u32[]{:S(2)}) collective-permute-start(bf16[80,512]{1,0:T(8,128)(2,1)S(1)} %get-tuple-element.351), channel_id=1, source_target_pairs={{0,8},{8,16},{16,24},{24,32},{32,40},{40,48},{48,56},{56,64},{64,7... | collective-permute-start | bytes 245768 | tf_op jit(solution)/shard_map/while/body/eval_jaxpr/ppermute | solution.py:16
  471.7 10.7 %collective-permute-start = (bf16[80,512]{1,0:T(8,128)(2,1)S(1)}, bf16[80,512]{1,0:T(8,128)(2,1)S(1)}, u32[]{:S(2)}, u32[]{:S(2)}) collective-permute-start(bf16[80,512]{1,0:T(8,128)(2,1)S(1)} %get-tuple-element.351), channel_id=1, source_target_pairs={{0,8},{8,16},{16,24},{24,32},{32,40},{40,48},{48,56},{56,64},{64,7... | collective-permute-start | bytes 245768 | tf_op jit(solution)/shard_map/while/body/eval_jaxpr/ppermute | solution.py:16
  485.0 11.2 %collective-permute-start = (bf16[80,512]{1,0:T(8,128)(2,1)S(1)}, bf16[80,512]{1,0:T(8,128)(2,1)S(1)}, u32[]{:S(2)}, u32[]{:S(2)}) collective-permute-start(bf16[80,512]{1,0:T(8,128)(2,1)S(1)} %get-tuple-element.351), channel_id=1, source_target_pairs={{0,8},{8,16},{16,24},{24,32},{32,40},{40,48},{48,56},{56,64},{64,7... | collective-permute-start | bytes 245768 | tf_op jit(solution)/shard_map/while/body/eval_jaxpr/ppermute | solution.py:16
  498.8 10.7 %collective-permute-start = (bf16[80,512]{1,0:T(8,128)(2,1)S(1)}, bf16[80,512]{1,0:T(8,128)(2,1)S(1)}, u32[]{:S(2)}, u32[]{:S(2)}) collective-permute-start(bf16[80,512]{1,0:T(8,128)(2,1)S(1)} %get-tuple-element.351), channel_id=1, source_target_pairs={{0,8},{8,16},{16,24},{24,32},{32,40},{40,48},{48,56},{56,64},{64,7... | collective-permute-start | bytes 245768 | tf_op jit(solution)/shard_map/while/body/eval_jaxpr/ppermute | solution.py:16
  512.1 11.1 %collective-permute-start = (bf16[80,512]{1,0:T(8,128)(2,1)S(1)}, bf16[80,512]{1,0:T(8,128)(2,1)S(1)}, u32[]{:S(2)}, u32[]{:S(2)}) collective-permute-start(bf16[80,512]{1,0:T(8,128)(2,1)S(1)} %get-tuple-element.351), channel_id=1, source_target_pairs={{0,8},{8,16},{16,24},{24,32},{32,40},{40,48},{48,56},{56,64},{64,7... | collective-permute-start | bytes 245768 | tf_op jit(solution)/shard_map/while/body/eval_jaxpr/ppermute | solution.py:16
  525.8 10.7 %collective-permute-start = (bf16[80,512]{1,0:T(8,128)(2,1)S(1)}, bf16[80,512]{1,0:T(8,128)(2,1)S(1)}, u32[]{:S(2)}, u32[]{:S(2)}) collective-permute-start(bf16[80,512]{1,0:T(8,128)(2,1)S(1)} %get-tuple-element.351), channel_id=1, source_target_pairs={{0,8},{8,16},{16,24},{24,32},{32,40},{40,48},{48,56},{56,64},{64,7... | collective-permute-start | bytes 245768 | tf_op jit(solution)/shard_map/while/body/eval_jaxpr/ppermute | solution.py:16
  539.1 11.2 %collective-permute-start = (bf16[80,512]{1,0:T(8,128)(2,1)S(1)}, bf16[80,512]{1,0:T(8,128)(2,1)S(1)}, u32[]{:S(2)}, u32[]{:S(2)}) collective-permute-start(bf16[80,512]{1,0:T(8,128)(2,1)S(1)} %get-tuple-element.351), channel_id=1, source_target_pairs={{0,8},{8,16},{16,24},{24,32},{32,40},{40,48},{48,56},{56,64},{64,7... | collective-permute-start | bytes 245768 | tf_op jit(solution)/shard_map/while/body/eval_jaxpr/ppermute | solution.py:16
  552.8 10.7 %collective-permute-start = (bf16[80,512]{1,0:T(8,128)(2,1)S(1)}, bf16[80,512]{1,0:T(8,128)(2,1)S(1)}, u32[]{:S(2)}, u32[]{:S(2)}) collective-permute-start(bf16[80,512]{1,0:T(8,128)(2,1)S(1)} %get-tuple-element.351), channel_id=1, source_target_pairs={{0,8},{8,16},{16,24},{24,32},{32,40},{40,48},{48,56},{56,64},{64,7... | collective-permute-start | bytes 245768 | tf_op jit(solution)/shard_map/while/body/eval_jaxpr/ppermute | solution.py:16
  566.1 10.7 %collective-permute-start = (bf16[80,512]{1,0:T(8,128)(2,1)S(1)}, bf16[80,512]{1,0:T(8,128)(2,1)S(1)}, u32[]{:S(2)}, u32[]{:S(2)}) collective-permute-start(bf16[80,512]{1,0:T(8,128)(2,1)S(1)} %get-tuple-element.351), channel_id=1, source_target_pairs={{0,8},{8,16},{16,24},{24,32},{32,40},{40,48},{48,56},{56,64},{64,7... | collective-permute-start | bytes 245768 | tf_op jit(solution)/shard_map/while/body/eval_jaxpr/ppermute | solution.py:16
  579.4 10.7 %collective-permute-start = (bf16[80,512]{1,0:T(8,128)(2,1)S(1)}, bf16[80,512]{1,0:T(8,128)(2,1)S(1)}, u32[]{:S(2)}, u32[]{:S(2)}) collective-permute-start(bf16[80,512]{1,0:T(8,128)(2,1)S(1)} %get-tuple-element.351), channel_id=1, source_target_pairs={{0,8},{8,16},{16,24},{24,32},{32,40},{40,48},{48,56},{56,64},{64,7... | collective-permute-start | bytes 245768 | tf_op jit(solution)/shard_map/while/body/eval_jaxpr/ppermute | solution.py:16
  685.7 11.2 %collective-permute-start = (bf16[80,512]{1,0:T(8,128)(2,1)S(1)}, bf16[80,512]{1,0:T(8,128)(2,1)S(1)}, u32[]{:S(2)}, u32[]{:S(2)}) collective-permute-start(bf16[80,512]{1,0:T(8,128)(2,1)S(1)} %get-tuple-element.351), channel_id=1, source_target_pairs={{0,8},{8,16},{16,24},{24,32},{32,40},{40,48},{48,56},{56,64},{64,7... | collective-permute-start | bytes 245768 | tf_op jit(solution)/shard_map/while/body/eval_jaxpr/ppermute | solution.py:16
  712.7 10.7 %collective-permute-start = (bf16[80,512]{1,0:T(8,128)(2,1)S(1)}, bf16[80,512]{1,0:T(8,128)(2,1)S(1)}, u32[]{:S(2)}, u32[]{:S(2)}) collective-permute-start(bf16[80,512]{1,0:T(8,128)(2,1)S(1)} %get-tuple-element.351), channel_id=1, source_target_pairs={{0,8},{8,16},{16,24},{24,32},{32,40},{40,48},{48,56},{56,64},{64,7... | collective-permute-start | bytes 245768 | tf_op jit(solution)/shard_map/while/body/eval_jaxpr/ppermute | solution.py:16
  832.3 10.7 %collective-permute-start = (bf16[80,512]{1,0:T(8,128)(2,1)S(1)}, bf16[80,512]{1,0:T(8,128)(2,1)S(1)}, u32[]{:S(2)}, u32[]{:S(2)}) collective-permute-start(bf16[80,512]{1,0:T(8,128)(2,1)S(1)} %get-tuple-element.351), channel_id=1, source_target_pairs={{0,8},{8,16},{16,24},{24,32},{32,40},{40,48},{48,56},{56,64},{64,7... | collective-permute-start | bytes 245768 | tf_op jit(solution)/shard_map/while/body/eval_jaxpr/ppermute | solution.py:16
  (150 other events, 1501.0 us)
Sparse Core Ops, SparseCore 0:
  9.5 39.9 all-gather.1
where the time goes:
time: 979 us; the launch traced here: 973 us
  waiting for transfers between devices  431 us (44%)
  starting transfers between devices  366 us (37%)
  blocking collectives  90.9 us (9%)
  local copies, waits for them, and re-layouts  57.2 us (6%)
  between operations  13.6 us (1%)
    ppermute x189, waiting for transfers between devices, passed_along(): return lax.ppermute(x, axis, [(i, (i + by) % count) for i in range(count)])  430 us
    ppermute x189, starting transfers between devices, passed_along(): return lax.ppermute(x, axis, [(i, (i + by) % count) for i in range(count)])  366 us
    psum x1, blocking collectives, per_device(): squares_total = lax.psum(squares_local, 'tp')  90.9 us
    dynamic_update_slice x192, local copies, waits for them, and re-layouts, deposit(): lax.dynamic_update_index_in_dim(store, piece, source, 0)  41.5 us
  transfers between devices with their start and end apart: 190, of which 126 were waited for; matrix products, arithmetic and copies ran while one was open for 5% of the time, Pallas kernels for 0%

commit v1 on v0

v1 whole, which is shorter than its diff:
```python
import jax
import jax.numpy as jnp
from jax import lax
from jax.experimental import pallas as pl
from jax.experimental.pallas import tpu as pltpu
from jax.sharding import PartitionSpec as P

D = 5120
HEAD = 128
TOK = 128
EPSILON = 1e-06
ROPE_BASE = 1000000.0
MESH = pl.DeviceIdType.MESH

NY, NZ, NX, NH, NK = 8, 2, 4, 4, 2
ROWS = 80
PART = NZ * ROWS
DEPTH = NY * PART
CHUNKS = 3
WIDE = 256
LOCAL = D // (NH * NK)
F32 = jnp.float32
BF16 = jnp.bfloat16


def kernel(
    hidden, segments, in_gain, q_gain, k_gain, w_query, w_key, w_value, out,
    hid, in_gain_v, segments_v, q_gain_v, k_gain_v, staged, h_t, h_n, weights, part_send, part_recv, part_own, squares, squares_all, heads,
    load_sem, zx_s, zx_r, y_s, y_r, y4_s, y4_r, xa_s, xa_r, hz_s, hz_r, hc_s, hc_r, sq_s, sq_r, pr_s, pr_r,
):
    chain, tp = lax.axis_index("chain"), lax.axis_index("tp")
    y, z, x = chain // (NZ * NX), (chain // NX) % NZ, chain % NX
    zh, core = tp // NK, tp % NK

    def at(y_=0, z_=0, x_=0, h_=0, k_=0):
        return {
            "chain": ((y + y_) % NY * NZ + (z + z_) % NZ) * NX + (x + x_) % NX,
            "tp": (zh + h_) % NH * NK + (core + k_) % NK,
        }

    def remote(src, dst, send, recv, to):
        return pltpu.make_async_remote_copy(
            src_ref=src, dst_ref=dst, send_sem=send, recv_sem=recv, device_id=to, device_id_type=MESH
        )

    def rows_of(y_):
        return ((y_ % NK) * NH + y_ // NK) * PART

    def block(y_, z_):
        return pl.ds(pl.multiple_of(rows_of(y_) + z_ * ROWS, 16), ROWS)

    mine = block(y, z)
    loads = [
        pltpu.make_async_copy(hidden, hid, load_sem.at[0]),
        pltpu.make_async_copy(w_key, weights.at[0, mine, pl.ds(0, HEAD)], load_sem.at[1]),
        pltpu.make_async_copy(w_value, weights.at[0, mine, pl.ds(HEAD, HEAD)], load_sem.at[2]),
        pltpu.make_async_copy(w_query.at[:, pl.ds(0, WIDE)], weights.at[1, mine], load_sem.at[3]),
        pltpu.make_async_copy(w_query.at[:, pl.ds(WIDE, WIDE)], weights.at[2, mine], load_sem.at[4]),
        pltpu.make_async_copy(in_gain, in_gain_v, load_sem.at[5]),
        pltpu.make_async_copy(segments, segments_v, load_sem.at[6]),
        pltpu.make_async_copy(q_gain, q_gain_v, load_sem.at[7]),
        pltpu.make_async_copy(k_gain, k_gain_v, load_sem.at[8]),
    ]
    for load in loads:
        load.start()

    partners = (
        [at(y_=1), at(y_=-1), at(z_=1), at(k_=1)]
        + [at(x_=i) for i in range(1, NX)]
        + [at(h_=i) for i in range(1, NH)]
    )
    barrier = pltpu.get_barrier_semaphore()
    for partner in partners:
        pl.semaphore_signal(barrier, inc=1, device_id=partner, device_id_type=MESH)

    loads[0].wait()
    loads[5].wait()
    raw = hid[...].astype(F32)
    gain = in_gain_v[0:1, pl.ds(pl.multiple_of(tp * LOCAL, 128), LOCAL)]
    turned = (raw * gain).T.astype(BF16)
    for i in range(NX):
        staged[i, :ROWS] = turned[i * ROWS : (i + 1) * ROWS]
        staged[i, ROWS:] = turned[(NX + i) * ROWS : (NX + i + 1) * ROWS]
    own_rows = pl.ds(pl.multiple_of(rows_of(tp), 16), PART)
    h_t[0, own_rows] = staged[x]
    square = jnp.sum(raw * raw, axis=1, keepdims=True)
    squares[0] = jnp.broadcast_to(square, (TOK, TOK)).T[:8]

    for load in loads[1:5] + loads[6:]:
        load.wait()
    pl.semaphore_wait(barrier, len(partners))

    zx = [
        remote(weights.at[c, mine], weights.at[c, mine], zx_s.at[c], zx_r.at[c], at(z_=1))
        for c in range(CHUNKS)
    ]

    def y_copy(c, step, p, right):
        origin = (y - (step - 1)) % NY if right else (y + (step - 1)) % NY
        region = weights.at[c, block(origin, (z + p) % NZ)]
        i = (c * 3 + step - 1) * 4 + p * 2 + (0 if right else 1)
        return remote(region, region, y_s.at[i], y_r.at[i], at(y_=1 if right else -1))

    def y_last(c, right):
        region = weights.at[c, block((y - 3) % NY, 0) if right else block((y + 3) % NY, 1)]
        i = c * 2 + (0 if right else 1)
        return remote(region, region, y4_s.at[i], y4_r.at[i], at(y_=1 if right else -1))

    def weights_step(c, step, p):
        for right in (True, False):
            if step > 1:
                y_copy(c, step - 1, p, right).wait_recv()
            y_copy(c, step, p, right).start()

    def weights_last(c):
        for p in range(NZ):
            for right in (True, False):
                y_copy(c, 3, p, right).wait_recv()
        for right in (True, False):
            y_last(c, right).start()

    to_x = {1: 1, 2: -1, 3: 2}
    xa = {
        q: remote(staged.at[(x + d) % NX], h_t.at[q, own_rows], xa_s.at[q - 1], xa_r.at[q - 1], at(x_=d))
        for q, d in to_x.items()
    }

    def hz_direct(q, right):
        region = h_t.at[q, own_rows]
        i = q * 4 + (0 if right else 1)
        return remote(region, region, hz_s.at[i], hz_r.at[i], at(h_=1 if right else -1))

    def hz_relay(q, right):
        source = (tp - NK) % (NH * NK) if right else (tp + NK) % (NH * NK)
        start = rows_of(source) + (0 if right else ROWS)
        region = h_t.at[q, pl.ds(pl.multiple_of(start, 16), ROWS)]
        i = q * 4 + (2 if right else 3)
        return remote(region, region, hz_s.at[i], hz_r.at[i], at(h_=1 if right else -1))

    def hz_start(q):
        if q > 0:
            xa[q].wait_recv()
        hz_direct(q, True).start()
        hz_direct(q, False).start()

    def hz_pass(q):
        hz_direct(q, True).wait_recv()
        hz_relay(q, True).start()
        hz_direct(q, False).wait_recv()
        hz_relay(q, False).start()

    half = pl.ds(pl.multiple_of(core * (NH * PART), 16), NH * PART)
    hc = [
        remote(h_t.at[q, half], h_t.at[q, half], hc_s.at[q], hc_r.at[q], at(k_=1)) for q in range(NX)
    ]

    def hc_start(q):
        hz_relay(q, True).wait_recv()
        hz_relay(q, False).wait_recv()
        hc[q].start()

    def turn(q):
        hc[q].wait_recv()
        h_n[pl.ds(q * TOK, TOK)] = h_t[q].T

    sq = [
        remote(squares.at[0], squares.at[i], sq_s.at[i], sq_r.at[i], at(h_=i)) for i in range(1, NH)
    ]
    sq_core = remote(squares_all.at[0], squares_all.at[1], sq_s.at[0], sq_r.at[0], at(k_=1))

    def project(c):
        y_last(c, True).wait_recv()
        y_last(c, False).wait_recv()
        total = jnp.dot(h_n[...], weights[c], preferred_element_type=F32)
        part_own[c] = total[:TOK]
        for q in range(1, NX):
            part_send[c, q - 1] = total[q * TOK : (q + 1) * TOK].astype(BF16)
        for q in (3, 1, 2):
            partial(c, q).start()

    def partial(c, q):
        back = {1: -1, 2: 1, 3: 2}[q]
        i = c * 3 + q - 1
        return remote(part_send.at[c, q - 1], part_recv.at[c, q - 1], pr_s.at[i], pr_r.at[i], at(x_=back))

    for c in range(CHUNKS):
        zx[c].start()
    for c in range(CHUNKS):
        weights_step(c, 1, 0)
    for q in (3, 1, 2):
        xa[q].start()
    hz_start(0)
    for copy in sq:
        copy.start()

    seg = jnp.broadcast_to(segments_v[...].astype(F32), (TOK, TOK))
    query_pos = lax.broadcasted_iota(jnp.int32, (TOK, TOK), 0)
    key_pos = lax.broadcasted_iota(jnp.int32, (TOK, TOK), 1)
    allowed = jnp.where((seg == seg.T) & (key_pos <= query_pos), 1.0, 0.0)
    offset = jnp.sum(allowed, axis=1, keepdims=True) - 1.0
    ladder = (key_pos % (HEAD // 2)).astype(F32)
    frequency = jnp.exp(ladder * (-2.0 / HEAD * 13.815510557964274))
    angle = offset * frequency
    heads[0] = jnp.cos(angle)
    heads[1] = jnp.sin(angle) * jnp.where(key_pos < HEAD // 2, -1.0, 1.0)
    heads[2] = allowed

    zx[0].wait_recv()
    weights_step(0, 1, 1)
    hz_start(1)
    hz_start(2)
    zx[1].wait_recv()
    weights_step(1, 1, 1)
    hz_start(3)
    zx[2].wait_recv()
    weights_step(2, 1, 1)
    for p in range(NZ):
        weights_step(0, 2, p)
    hz_pass(0)
    for p in range(NZ):
        weights_step(1, 2, p)
    hz_pass(1)
    for p in range(NZ):
        weights_step(2, 2, p)
    hz_pass(2)
    for p in range(NZ):
        weights_step(0, 3, p)
    hz_pass(3)
    hc_start(0)
    for p in range(NZ):
        weights_step(1, 3, p)
    hc_start(1)
    turn(0)
    for p in range(NZ):
        weights_step(2, 3, p)
    hc_start(2)
    turn(1)
    weights_last(0)
    hc_start(3)
    turn(2)
    weights_last(1)
    for copy in sq:
        copy.wait_recv()
    squares_all[0] = (squares[0] + squares[1]) + (squares[2] + squares[3])
    sq_core.start()
    turn(3)
    weights_last(2)
    for c in range(CHUNKS):
        project(c)
    sq_core.wait_recv()
    token_squares = jnp.broadcast_to((squares_all[0] + squares_all[1])[:1], (TOK, TOK)).T
    inverse = lax.rsqrt(token_squares / D + EPSILON)

    def gathered(c):
        for q in range(1, NX):
            partial(c, q).wait_recv()
        total = part_own[c]
        for q in range(1, NX):
            total = total + part_recv[c, q - 1].astype(F32)
        return total[:, :HEAD] * inverse, total[:, HEAD:] * inverse

    def rotated(values, gain):
        mean = jnp.mean(values * values, axis=1, keepdims=True)
        normed = values * lax.rsqrt(mean + EPSILON) * gain
        return (normed * heads[0] + pltpu.roll(normed, HEAD // 2, 1) * heads[1]).astype(BF16)

    keys, values = gathered(0)
    keys = rotated(keys, k_gain_v[...])
    values = values.astype(BF16)
    for c in range(1, CHUNKS):
        for i, query in enumerate(gathered(c)):
            query = rotated(query, q_gain_v[...])
            logits = lax.dot_general(query, keys, (((1,), (1,)), ((), ())), preferred_element_type=F32)
            expo = jnp.where(heads[2] > 0.5, jnp.exp(logits * HEAD**-0.5), 0.0)
            attend = (expo / jnp.sum(expo, axis=1, keepdims=True)).astype(BF16)
            context = jnp.dot(attend, values, preferred_element_type=F32).astype(BF16)
            out[:, pl.ds(((c - 1) * 2 + i) * HEAD, HEAD)] = context

    for c in range(CHUNKS):
        zx[c].wait_send()
        for right in (True, False):
            for p in range(NZ):
                for step in (1, 2, 3):
                    y_copy(c, step, p, right).wait_send()
            y_last(c, right).wait_send()
        for q in range(1, NX):
            partial(c, q).wait_send()
    for q in range(NX):
        if q:
            xa[q].wait_send()
        for right in (True, False):
            hz_direct(q, right).wait_send()
            hz_relay(q, right).wait_send()
        hc[q].wait_send()
    for copy in sq:
        copy.wait_send()
    sq_core.wait_send()


def per_device(hidden, segments, in_gain, q_gain, k_gain, w_query, w_key, w_value):
    vmem = pl.BlockSpec(memory_space=pltpu.VMEM)
    hbm = pl.BlockSpec(memory_space=pl.ANY)
    dma = pltpu.SemaphoreType.DMA
    return pl.pallas_call(
        kernel,
        name="layer",
        out_shape=jax.ShapeDtypeStruct((TOK, 4 * HEAD), BF16),
        in_specs=[hbm] * 8,
        out_specs=vmem,
        scratch_shapes=[
            pltpu.VMEM((TOK, LOCAL), BF16),
            pltpu.VMEM((1, D), F32),
            pltpu.VMEM((1, TOK), jnp.int32),
            pltpu.VMEM((1, HEAD), F32),
            pltpu.VMEM((1, HEAD), F32),
            pltpu.VMEM((NX, PART, TOK), BF16),
            pltpu.VMEM((NX, DEPTH, TOK), BF16),
            pltpu.VMEM((NX * TOK, DEPTH), BF16),
            pltpu.VMEM((CHUNKS, DEPTH, WIDE), BF16),
            pltpu.VMEM((CHUNKS, NX - 1, TOK, WIDE), BF16),
            pltpu.VMEM((CHUNKS, NX - 1, TOK, WIDE), BF16),
            pltpu.VMEM((CHUNKS, TOK, WIDE), F32),
            pltpu.VMEM((NH, 8, TOK), F32),
            pltpu.VMEM((2, 8, TOK), F32),
            pltpu.VMEM((3, TOK, TOK), F32),
            dma((9,)),
            dma((CHUNKS,)), dma((CHUNKS,)),
            dma((CHUNKS * 12,)), dma((CHUNKS * 12,)),
            dma((CHUNKS * 2,)), dma((CHUNKS * 2,)),
            dma((NX - 1,)), dma((NX - 1,)),
            dma((NX * 4,)), dma((NX * 4,)),
            dma((NX,)), dma((NX,)),
            dma((NH,)), dma((NH,)),
            dma((CHUNKS * 3,)), dma((CHUNKS * 3,)),
        ],
        compiler_params=pltpu.CompilerParams(
            collective_id=0, has_side_effects=True, vmem_limit_bytes=64 * 2**20
        ),
    )(
        hidden,
        segments.reshape(1, TOK),
        in_gain.reshape(1, D),
        q_gain.reshape(1, HEAD),
        k_gain.reshape(1, HEAD),
        w_query,
        w_key,
        w_value,
    )


def solution(mesh):
    placed = (
        P("chain", "tp"), P("chain"), P(), P(), P(), P("chain", "tp"), P("chain", "tp"), P("chain", "tp"),
    )
    return jax.shard_map(
        per_device, mesh=mesh, in_specs=placed, out_specs=P("chain", "tp"), check_vma=False
    )
```

time: 979 us -> 51.5 us (0.05)
  waiting for transfers between devices: 431 us -> 0 us
  starting transfers between devices: 366 us -> 0 us
  blocking collectives: 90.9 us -> 0 us
  local copies, waits for them, and re-layouts: 57.2 us -> 1.57 us
  Pallas kernels: 0 us -> 49.8 us
  between operations: 13.6 us -> 0.01 us
    ppermute x189 -> x0, waiting for transfers between devices: 430 us -> none  [passed_along(): return lax.ppermute(x, axis, [(i, (i + by) % count) for i in range(count)])]
    ppermute x189 -> x0, starting transfers between devices: 366 us -> none  [passed_along(): return lax.ppermute(x, axis, [(i, (i + by) % count) for i in range(count)])]
    psum x1 -> x0, blocking collectives: 90.9 us -> none  [per_device(): squares_total = lax.psum(squares_local, 'tp')]
    pallas_call x0 -> x1, Pallas kernels: none -> 49.8 us  [per_device(): pl.pallas_call(kernel, name='layer', out_shape=jax.ShapeDtypeStruct((TOK,...]
    dynamic_update_slice x192 -> x0, local copies, waits for them, and re-layouts: 41.5 us -> none  [deposit(): lax.dynamic_update_index_in_dim(store, piece, source, 0)]
  transfers between devices with their start and end apart: 190 -> 0, of which waited for: 126 -> 0; matrix products, arithmetic and copies ran while one was open for 5% -> 0% of each run, Pallas kernels for 0% -> 0%
where the time goes in v1:
time: 51.5 us; the launch traced here: 51.3 us
  Pallas kernels  49.8 us (97%)
  local copies, waits for them, and re-layouts  1.57 us (3%)
    pallas_call x1, Pallas kernels, per_device(): pl.pallas_call(kernel, name='layer', out_shape=jax.ShapeDtypeStruct((TOK,...  49.8 us
    unnamed x1, local copies, waits for them, and re-layouts  1.57 us

profile of v1, /device:TPU:1, one launch (start us, length us, event | category | flops | bytes accessed | tf_op | source)
XLA Modules:
  0.0 51.3 jit_solution(1488561441407581201)
XLA Ops:
  0.0 49.8 %layer.1 = bf16[128,512]{1,0:T(8,128)(2,1)} custom-call(bf16[128,640]{1,0:T(8,128)(2,1)} %hidden.1, s32[1,128]{1,0:T(1,128)} %bitcast.5, f32[1,5120]{1,0:T(1,128)} %bitcast.4, f32[1,128]{1,0:T(1,128)} %bitcast.6, f32[1,128]{1,0:T(1,128)} %bitcast.7, bf16[80,512]{1,0:T(8,128)(2,1)} %w_query.1, bf16[80,128]{1,0:T(8,128)(2,1)} %w_key.1, bf16[80,128]{1,0:T(8,128)(2,1)} %w_value.1), custom_call_target="tpu_custom_call" | custom-call | tf_op jit(solution)/shard_map/layer/pallas_call | solution.py:304
  49.8 1.6 %copy.10 = bf16[128,512]{1,0:T(8,128)(2,1)} copy(bf16[128,512]{1,0:T(8,128)(2,1)} %layer.1) | data formatting | bytes 262144

commit v2 on v1

v2 whole, which is shorter than its diff:
```python
import jax
import jax.numpy as jnp
from jax import lax
from jax.experimental import pallas as pl
from jax.experimental.pallas import tpu as pltpu
from jax.sharding import PartitionSpec as P

D = 5120
HEAD = 128
TOK = 128
EPSILON = 1e-06
ROPE_BASE = 1000000.0
MESH = pl.DeviceIdType.MESH

NY, NZ, NX, NH, NK = 8, 2, 4, 4, 2
ROWS = 80
PART = NZ * ROWS
DEPTH = NY * PART
CHUNKS = (2, 2, 2)
ROUTES = {(3, True): (0, 0), (1, False): (0, 160), (0, True): (0, 160), (2, False): (0, 0)}
PAIR, STEP, LAST, SWAP, SEND, PASS, CORE, TURN, PROJECT, DONE, SQUARES, SUM, SCALE, TABLES, MEET = range(15)
ORDER_0 = (
    (PAIR, 0), (PAIR, 1), (PAIR, 2), (SWAP, 3), (SWAP, 1), (SWAP, 2), (STEP, 0, 1, 0), (STEP, 1, 1, 0),
    (STEP, 2, 1, 0), (STEP, 0, 1, 1), (STEP, 1, 1, 1), (STEP, 0, 2, 0), (STEP, 2, 1, 1), (STEP, 1, 2, 0), (MEET, 1),
    (SEND, 3, True), (SEND, 1, True), (SEND, 2, True), (STEP, 0, 2, 1), (STEP, 1, 2, 1), (STEP, 2, 2, 0), (MEET, 2),
    (STEP, 2, 2, 1), (MEET, 3), (SEND, 3, False), (SEND, 1, False), (SEND, 2, False), (PASS, 0, False), (SQUARES,),
    (STEP, 0, 3, 0), (TABLES,), (STEP, 0, 3, 1), (PASS, 3, False), (STEP, 1, 3, 0), (STEP, 1, 3, 1),
    (PASS, 0, True), (PASS, 1, False), (STEP, 2, 3, 0), (STEP, 2, 3, 1), (PASS, 3, True), (PASS, 2, False),
    (LAST, 0), (LAST, 1), (PASS, 1, True), (SEND, 0, False), (LAST, 2), (PASS, 2, True), (SUM,), (CORE, 3),
    (SCALE,), (CORE, 0), (TURN, 3), (CORE, 1), (SEND, 0, True), (PROJECT, 0, 3), (TURN, 0), (PROJECT, 1, 3),
    (CORE, 2), (TURN, 1), (PROJECT, 0, 1), (PROJECT, 1, 1), (PROJECT, 2, 3), (TURN, 2), (PROJECT, 0, 2),
    (PROJECT, 1, 2), (PROJECT, 2, 1), (PROJECT, 2, 2), (PROJECT, 0, 0), (PROJECT, 1, 0), (PROJECT, 2, 0), (DONE, 0),
    (DONE, 1), (DONE, 2),
)
ORDER_1 = (
    (PAIR, 0), (PAIR, 1), (PAIR, 2), (SWAP, 3), (SWAP, 1), (SWAP, 2), (STEP, 0, 1, 0), (STEP, 1, 1, 0),
    (STEP, 2, 1, 0), (SEND, 0, False), (STEP, 0, 1, 1), (STEP, 1, 1, 1), (SEND, 3, False), (SEND, 1, False),
    (SEND, 2, False), (STEP, 0, 2, 0), (STEP, 2, 1, 1), (STEP, 1, 2, 0), (MEET, 1), (SEND, 3, True),
    (SEND, 1, True), (SEND, 2, True), (STEP, 0, 2, 1), (MEET, 2), (SQUARES,), (STEP, 1, 2, 1), (PASS, 3, True),
    (STEP, 2, 2, 0), (STEP, 2, 2, 1), (PASS, 1, True), (TABLES,), (PASS, 0, False), (STEP, 0, 3, 0),
    (STEP, 0, 3, 1), (PASS, 3, False), (PASS, 2, True), (STEP, 1, 3, 0), (STEP, 1, 3, 1), (PASS, 1, False),
    (SEND, 0, True), (STEP, 2, 3, 0), (STEP, 2, 3, 1), (PASS, 2, False), (LAST, 0), (SUM,), (LAST, 1), (SCALE,),
    (LAST, 2), (CORE, 3), (TURN, 3), (CORE, 1), (PROJECT, 0, 3), (PROJECT, 1, 3), (PROJECT, 2, 3), (TURN, 1),
    (CORE, 2), (PROJECT, 0, 1), (PROJECT, 1, 1), (PROJECT, 2, 1), (TURN, 2), (PASS, 0, True), (CORE, 0),
    (PROJECT, 0, 2), (PROJECT, 1, 2), (PROJECT, 2, 2), (TURN, 0), (PROJECT, 0, 0), (PROJECT, 1, 0), (PROJECT, 2, 0),
    (DONE, 0), (DONE, 1), (DONE, 2),
)
ORDER_2 = (
    (PAIR, 0), (SWAP, 3), (SWAP, 1), (SWAP, 2), (PAIR, 1), (STEP, 0, 1, 0), (PAIR, 2), (STEP, 1, 1, 0),
    (STEP, 2, 1, 0), (SEND, 0, False), (STEP, 0, 1, 1), (SEND, 3, False), (STEP, 1, 1, 1), (SEND, 1, False),
    (SEND, 2, False), (MEET, 1), (SEND, 3, True), (SEND, 1, True), (SEND, 2, True), (SQUARES,), (STEP, 2, 1, 1),
    (STEP, 0, 2, 0), (STEP, 1, 2, 0), (STEP, 0, 2, 1), (STEP, 1, 2, 1), (PASS, 3, True), (PASS, 0, False),
    (STEP, 2, 2, 0), (STEP, 2, 2, 1), (PASS, 1, True), (TABLES,), (PASS, 3, False), (STEP, 0, 3, 0),
    (SEND, 0, True), (STEP, 0, 3, 1), (PASS, 2, True), (PASS, 1, False), (STEP, 1, 3, 0), (STEP, 1, 3, 1),
    (PASS, 2, False), (STEP, 2, 3, 0), (CORE, 3), (STEP, 2, 3, 1), (CORE, 1), (LAST, 0), (TURN, 3), (CORE, 2),
    (PASS, 0, True), (SUM,), (TURN, 1), (LAST, 1), (TURN, 2), (SCALE,), (LAST, 2), (PROJECT, 0, 3), (PROJECT, 0, 1),
    (PROJECT, 0, 2), (PROJECT, 1, 3), (PROJECT, 1, 1), (PROJECT, 1, 2), (PROJECT, 2, 3), (PROJECT, 2, 1),
    (PROJECT, 2, 2), (CORE, 0), (TURN, 0), (PROJECT, 0, 0), (PROJECT, 1, 0), (PROJECT, 2, 0), (DONE, 0), (DONE, 1),
    (DONE, 2),
)
ORDER_3 = (
    (PAIR, 0), (SWAP, 3), (SWAP, 1), (SWAP, 2), (PAIR, 1), (SQUARES,), (PAIR, 2), (STEP, 0, 1, 0), (STEP, 1, 1, 0),
    (SEND, 0, True), (SEND, 0, False), (STEP, 2, 1, 0), (STEP, 0, 1, 1), (SEND, 3, True), (SEND, 3, False),
    (SEND, 1, True), (SEND, 1, False), (SEND, 2, True), (SEND, 2, False), (STEP, 1, 1, 1), (STEP, 2, 1, 1),
    (STEP, 0, 2, 0), (STEP, 1, 2, 0), (STEP, 0, 2, 1), (PASS, 3, False), (PASS, 3, True), (STEP, 1, 2, 1),
    (STEP, 2, 2, 0), (PASS, 1, False), (PASS, 1, True), (TABLES,), (STEP, 2, 2, 1), (STEP, 0, 3, 0),
    (PASS, 2, False), (PASS, 2, True), (STEP, 0, 3, 1), (STEP, 1, 3, 0), (SUM,), (CORE, 3), (STEP, 1, 3, 1),
    (CORE, 1), (STEP, 2, 3, 0), (SCALE,), (TURN, 3), (PASS, 0, True), (STEP, 2, 3, 1), (TURN, 1), (CORE, 2),
    (LAST, 0), (PASS, 0, False), (LAST, 1), (TURN, 2), (CORE, 0), (LAST, 2), (PROJECT, 0, 3), (TURN, 0),
    (PROJECT, 0, 1), (PROJECT, 0, 2), (PROJECT, 1, 3), (PROJECT, 1, 1), (PROJECT, 1, 2), (PROJECT, 2, 3),
    (PROJECT, 2, 1), (PROJECT, 2, 2), (PROJECT, 0, 0), (PROJECT, 1, 0), (PROJECT, 2, 0), (DONE, 0), (DONE, 1),
    (DONE, 2),
)
ORDERS = (ORDER_0, ORDER_1, ORDER_2, ORDER_3)
LOCAL = D // (NH * NK)
F32 = jnp.float32
BF16 = jnp.bfloat16


def kernel(*refs):
    hidden, segments, in_gain, q_gain, k_gain, w_query, w_key, w_value, out = refs[:9]
    hid, in_gain_v, segments_v, q_gain_v, k_gain_v, staged, h_t, h_n, squares, squares_all, heads = refs[9:20]
    load_sem, zx_s, zx_r, y_s, y_r, y4_s, y4_r, xa_s, xa_r, hz_s, hz_r, hc_s, hc_r, sq_s, sq_r, pr_s, pr_r, ready = refs[20:38]
    count = len(CHUNKS)
    weights, part_send, part_recv, part_own = (refs[38 + i * count : 38 + (i + 1) * count] for i in range(4))
    chain, tp = lax.axis_index("chain"), lax.axis_index("tp")
    y, z, x = chain // (NZ * NX), (chain // NX) % NZ, chain % NX
    zh, core = tp // NK, tp % NK

    def at(y_=0, z_=0, x_=0, h_=0, k_=0):
        return {
            "chain": ((y + y_) % NY * NZ + (z + z_) % NZ) * NX + (x + x_) % NX,
            "tp": (zh + h_) % NH * NK + (core + k_) % NK,
        }

    def remote(src, dst, send, recv, to):
        return pltpu.make_async_remote_copy(
            src_ref=src, dst_ref=dst, send_sem=send, recv_sem=recv, device_id=to, device_id_type=MESH
        )

    def rows_of(y_):
        return ((y_ % NK) * NH + y_ // NK) * PART

    def block(y_, z_):
        return pl.ds(pl.multiple_of(rows_of(y_) + z_ * ROWS, 16), ROWS)

    state, swapped = {}, set()
    partners = (
        [at(y_=1), at(y_=-1), at(z_=1), at(k_=1)] + [at(x_=i) for i in range(1, NX)]
    )
    barrier = pltpu.get_barrier_semaphore()
    for partner in partners:
        pl.semaphore_signal(barrier, inc=1, device_id=partner, device_id_type=MESH)
    for i in range(1, NH):

        @pl.when(zh + i < NH)
        def _():
            pl.semaphore_signal(barrier, inc=1, device_id=at(h_=i), device_id_type=MESH)


    mine = block(y, z)
    loads = [
        pltpu.make_async_copy(hidden, hid, load_sem.at[0]),
        pltpu.make_async_copy(in_gain, in_gain_v, load_sem.at[1]),
        pltpu.make_async_copy(segments, segments_v, load_sem.at[2]),
        pltpu.make_async_copy(q_gain, q_gain_v, load_sem.at[3]),
        pltpu.make_async_copy(k_gain, k_gain_v, load_sem.at[4]),
    ]
    columns = [w_key, w_value] + [w_query.at[:, pl.ds(i * HEAD, HEAD)] for i in range(4)]
    place = [(c, i) for c, wide in enumerate(CHUNKS) for i in range(wide)]
    for i, (source, (c, j)) in enumerate(zip(columns, place)):
        target = weights[c].at[mine, pl.ds(j * HEAD, HEAD)]
        loads.append(pltpu.make_async_copy(source, target, load_sem.at[5 + i]))
    for load in loads:
        load.start()

    loads[0].wait()
    loads[1].wait()
    raw = hid[...].astype(F32)
    gain = in_gain_v[0:1, pl.ds(pl.multiple_of(tp * LOCAL, 128), LOCAL)]
    turned = (raw * gain).T.astype(BF16)
    for i in range(NX):
        staged[i, :ROWS] = turned[i * ROWS : (i + 1) * ROWS]
        staged[i, ROWS:] = turned[(NX + i) * ROWS : (NX + i + 1) * ROWS]
    own_rows = pl.ds(pl.multiple_of(rows_of(tp), 16), PART)
    h_t[0, own_rows] = staged[x]
    square = jnp.sum(raw * raw, axis=1, keepdims=True)
    squares[0] = jnp.broadcast_to(square, (TOK, TOK)).T[:8]

    for load in loads[2:]:
        load.wait()
    pl.semaphore_wait(barrier, len(partners) + zh)
    for i in range(1, NH):

        @pl.when(zh >= i)
        def _():
            pl.semaphore_signal(ready.at[i], inc=1, device_id=at(h_=-i), device_id_type=MESH)


    zx = [
        remote(weights[c].at[mine], weights[c].at[mine], zx_s.at[c], zx_r.at[c], at(z_=1))
        for c in range(count)
    ]

    def y_copy(c, step, p, right):
        origin = (y - (step - 1)) % NY if right else (y + (step - 1)) % NY
        region = weights[c].at[block(origin, (z + p) % NZ)]
        i = (c * 3 + step - 1) * 4 + p * 2 + (0 if right else 1)
        return remote(region, region, y_s.at[i], y_r.at[i], at(y_=1 if right else -1))

    def y_last(c, right):
        region = weights[c].at[block((y - 3) % NY, 0) if right else block((y + 3) % NY, 1)]
        i = c * 2 + (0 if right else 1)
        return remote(region, region, y4_s.at[i], y4_r.at[i], at(y_=1 if right else -1))

    def weights_step(c, step, p):
        for right in (True, False):
            if step > 1:
                y_copy(c, step - 1, p, right).wait_recv()
            y_copy(c, step, p, right).start()

    def weights_last(c):
        for p in range(NZ):
            for right in (True, False):
                y_copy(c, 3, p, right).wait_recv()
        for right in (True, False):
            y_last(c, right).start()

    to_x = {1: 1, 2: -1, 3: 2}
    xa = {
        q: remote(staged.at[(x + d) % NX], h_t.at[q, own_rows], xa_s.at[q - 1], xa_r.at[q - 1], at(x_=d))
        for q, d in to_x.items()
    }

    def hz_direct(q, right):
        region = h_t.at[q, own_rows]
        i = q * 4 + (0 if right else 1)
        return remote(region, region, hz_s.at[i], hz_r.at[i], at(h_=1 if right else -1))

    def route(here, right):
        return ROUTES.get((here, right), (0, ROWS) if right else (ROWS, ROWS))

    def hz_relay(q, right, here):
        first, amount = route(here, right)
        source = (tp - NK) % (NH * NK) if right else (tp + NK) % (NH * NK)
        region = h_t.at[q, pl.ds(pl.multiple_of(rows_of(source) + first, 16), amount)]
        i = q * 4 + (2 if right else 3)
        return remote(region, region, hz_s.at[i], hz_r.at[i], at(h_=1 if right else -1))

    def hz_arriving(q, right, here):
        first, amount = route((here - 1) % NH if right else (here + 1) % NH, right)
        if amount:
            source = (tp - 2 * NK) % (NH * NK)
            region = h_t.at[q, pl.ds(pl.multiple_of(rows_of(source) + first, 16), amount)]
            i = q * 4 + (2 if right else 3)
            remote(region, region, hz_s.at[i], hz_r.at[i], at(h_=1 if right else -1)).wait_recv()

    def hz_start(q, right):
        if q > 0 and q not in swapped:
            swapped.add(q)
            xa[q].wait_recv()
        hz_direct(q, right).start()

    def hz_pass(q, right):
        hz_direct(q, right).wait_recv()
        if route(state["here"], right)[1]:
            hz_relay(q, right, state["here"]).start()

    def meet(i):
        pl.semaphore_wait(ready.at[i], 1)

    half = pl.ds(pl.multiple_of(core * (NH * PART), 16), NH * PART)
    hc = [
        remote(h_t.at[q, half], h_t.at[q, half], hc_s.at[q], hc_r.at[q], at(k_=1)) for q in range(NX)
    ]

    def hc_start(q):
        for right in (True, False):
            hz_arriving(q, right, state["here"])
        hc[q].start()

    def turn(q):
        hc[q].wait_recv()
        h_n[pl.ds(q * TOK, TOK)] = h_t[q].T

    sq = [
        remote(squares.at[0], squares.at[i], sq_s.at[i], sq_r.at[i], at(h_=i)) for i in range(1, NH)
    ]
    sq_core = remote(squares_all.at[0], squares_all.at[1], sq_s.at[0], sq_r.at[0], at(k_=1))

    def arrived(c):
        y_last(c, True).wait_recv()
        y_last(c, False).wait_recv()

    def project(c, first, last):
        total = jnp.dot(h_n[pl.ds(first * TOK, (last - first) * TOK)], weights[c][...], preferred_element_type=F32)
        for q in range(first, last):
            piece = total[(q - first) * TOK : (q - first + 1) * TOK]
            if q == 0:
                part_own[c][...] = piece
            else:
                part_send[c][q - 1] = piece.astype(BF16)
        for q in range(last - 1, max(first, 1) - 1, -1):
            partial(c, q).start()

    def partial(c, q):
        back = {1: -1, 2: 1, 3: 2}[q]
        i = c * 3 + q - 1
        return remote(part_send[c].at[q - 1], part_recv[c].at[q - 1], pr_s.at[i], pr_r.at[i], at(x_=back))

    def add_squares():
        for copy in sq:
            copy.wait_recv()
        squares_all[0] = (squares[0] + squares[1]) + (squares[2] + squares[3])
        sq_core.start()

    def scale_squares():
        sq_core.wait_recv()
        token_squares = jnp.broadcast_to((squares_all[0] + squares_all[1])[:1], (TOK, TOK)).T
        heads[3] = lax.rsqrt(token_squares / D + EPSILON)

    def rotated(values, gain):
        mean = jnp.mean(values * values, axis=1, keepdims=True)
        normed = values * lax.rsqrt(mean + EPSILON) * gain
        return (normed * heads[0] + pltpu.roll(normed, HEAD // 2, 1) * heads[1]).astype(BF16)

    key_value = {}

    def finish(c):
        for q in range(1, NX):
            partial(c, q).wait_recv()
        total = part_own[c][...]
        for q in range(1, NX):
            total = total + part_recv[c][q - 1].astype(F32)
        for i, place_ in enumerate(place):
            if place_[0] != c:
                continue
            columns_ = total[:, place_[1] * HEAD : (place_[1] + 1) * HEAD] * heads[3]
            if i == 0:
                key_value[0] = rotated(columns_, k_gain_v[...])
            elif i == 1:
                key_value[1] = columns_.astype(BF16)
            else:
                attention(i - 2, rotated(columns_, q_gain_v[...]))

    def attention(head, query):
        logits = lax.dot_general(query, key_value[0], (((1,), (1,)), ((), ())), preferred_element_type=F32)
        expo = jnp.where(heads[2] > 0.5, jnp.exp(logits * HEAD**-0.5), 0.0)
        attend = (expo / jnp.sum(expo, axis=1, keepdims=True)).astype(BF16)
        context = jnp.dot(attend, key_value[1], preferred_element_type=F32).astype(BF16)
        out[:, pl.ds(head * HEAD, HEAD)] = context

    def tables():
        seg = jnp.broadcast_to(segments_v[...].astype(F32), (TOK, TOK))
        query_pos = lax.broadcasted_iota(jnp.int32, (TOK, TOK), 0)
        key_pos = lax.broadcasted_iota(jnp.int32, (TOK, TOK), 1)
        allowed = jnp.where((seg == seg.T) & (key_pos <= query_pos), 1.0, 0.0)
        offset = jnp.sum(allowed, axis=1, keepdims=True) - 1.0
        ladder = (key_pos % (HEAD // 2)).astype(F32)
        frequency = jnp.exp(ladder * (-2.0 / HEAD * 13.815510557964274))
        angle = offset * frequency
        heads[0] = jnp.cos(angle)
        heads[1] = jnp.sin(angle) * jnp.where(key_pos < HEAD // 2, -1.0, 1.0)
        heads[2] = allowed

    begun = set()

    def project_part(c, q):
        if c not in begun:
            begun.add(c)
            arrived(c)
        project(c, q, q + 1)

    def start_squares():
        for copy in sq:
            copy.start()

    def weights_step_from(c, step, p):
        if step == 1 and p == 1:
            zx[c].wait_recv()
        weights_step(c, step, p)

    actions = {
        PAIR: lambda c: zx[c].start(),
        STEP: weights_step_from,
        LAST: weights_last,
        SWAP: lambda q: xa[q].start(),
        SEND: hz_start,
        PASS: hz_pass,
        CORE: hc_start,
        TURN: turn,
        MEET: meet,
        PROJECT: project_part,
        DONE: finish,
        SQUARES: start_squares,
        SUM: add_squares,
        SCALE: scale_squares,
        TABLES: tables,
    }
    def left(here):
        for c in range(count):
            zx[c].wait_send()
            for right in (True, False):
                for p in range(NZ):
                    for step in (1, 2, 3):
                        y_copy(c, step, p, right).wait_send()
                y_last(c, right).wait_send()
        for q in range(NX):
            if q:
                xa[q].wait_send()
            for right in (True, False):
                hz_direct(q, right).wait_send()
            hc[q].wait_send()
        for copy in sq:
            copy.wait_send()
        sq_core.wait_send()
        for q in range(NX):
            for right in (True, False):
                if route(here, right)[1]:
                    hz_relay(q, right, here).wait_send()

    def run(here, order):
        state["here"] = here
        begun.clear()
        key_value.clear()
        swapped.clear()
        for name, *numbers in order:
            if (name, *numbers) == (DONE, 0):
                left(here)
            actions[name](*numbers)
        for c in range(count):
            for q in range(1, NX):
                partial(c, q).wait_send()

    for here, order in enumerate(ORDERS):
        pl.when(zh == here)(lambda here=here, order=order: run(here, order))


def per_device(hidden, segments, in_gain, q_gain, k_gain, w_query, w_key, w_value):
    vmem = pl.BlockSpec(memory_space=pltpu.VMEM)
    hbm = pl.BlockSpec(memory_space=pltpu.HBM)
    dma = pltpu.SemaphoreType.DMA
    count, widths = len(CHUNKS), [wide * HEAD for wide in CHUNKS]
    return pl.pallas_call(
        kernel,
        name="layer",
        out_shape=jax.ShapeDtypeStruct((TOK, 4 * HEAD), BF16),
        in_specs=[hbm] * 8,
        out_specs=vmem,
        scratch_shapes=[
            pltpu.VMEM((TOK, LOCAL), BF16),
            pltpu.VMEM((1, D), F32),
            pltpu.VMEM((1, TOK), jnp.int32),
            pltpu.VMEM((1, HEAD), F32),
            pltpu.VMEM((1, HEAD), F32),
            pltpu.VMEM((NX, PART, TOK), BF16),
            pltpu.VMEM((NX, DEPTH, TOK), BF16),
            pltpu.VMEM((NX * TOK, DEPTH), BF16),
            pltpu.VMEM((NH, 8, TOK), F32),
            pltpu.VMEM((2, 8, TOK), F32),
            pltpu.VMEM((4, TOK, TOK), F32),
            dma((11,)),
            dma((count,)), dma((count,)),
            dma((count * 12,)), dma((count * 12,)),
            dma((count * 2,)), dma((count * 2,)),
            dma((NX - 1,)), dma((NX - 1,)),
            dma((NX * 4,)), dma((NX * 4,)),
            dma((NX,)), dma((NX,)),
            dma((NH,)), dma((NH,)),
            dma((count * 3,)), dma((count * 3,)),
            pltpu.SemaphoreType.REGULAR((NH,)),
            *[pltpu.VMEM((DEPTH, wide), BF16) for wide in widths],
            *[pltpu.VMEM((NX - 1, TOK, wide), BF16) for wide in widths],
            *[pltpu.VMEM((NX - 1, TOK, wide), BF16) for wide in widths],
            *[pltpu.VMEM((TOK, wide), F32) for wide in widths],
        ],
        compiler_params=pltpu.CompilerParams(
            collective_id=0, has_side_effects=True, vmem_limit_bytes=64 * 2**20
        ),
    )(
        hidden,
        segments.reshape(1, TOK),
        in_gain.reshape(1, D),
        q_gain.reshape(1, HEAD),
        k_gain.reshape(1, HEAD),
        w_query,
        w_key,
        w_value,
    )


def solution(mesh):
    placed = (
        P("chain", "tp"), P("chain"), P(), P(), P(), P("chain", "tp"), P("chain", "tp"), P("chain", "tp"),
    )
    return jax.shard_map(
        per_device, mesh=mesh, in_specs=placed, out_specs=P("chain", "tp"), check_vma=False
    )
```

time: 51.5 us -> 43.8 us (0.85); the launches traced: 51.3 us -> 43.1 us
  Pallas kernels: 49.8 us -> 41.5 us
    pallas_call x1, Pallas kernels: 49.8 us -> 41.5 us  [per_device(): pl.pallas_call(kernel, name='layer', out_shape=jax.ShapeDtypeStruct((TOK,...]
where the time goes in v2:
time: 43.8 us; the launch traced here: 43.1 us
  Pallas kernels  41.5 us (95%)
  local copies, waits for them, and re-layouts  1.57 us (4%)
    pallas_call x1, Pallas kernels, per_device(): pl.pallas_call(kernel, name='layer', out_shape=jax.ShapeDtypeStruct((TOK,...  41.5 us
    unnamed x1, local copies, waits for them, and re-layouts  1.57 us

profile of v2, /device:TPU:1, one launch (start us, length us, event | category | flops | bytes accessed | tf_op | source)
XLA Modules:
  0.0 43.1 jit_solution(9008814535137259916)
XLA Ops:
  0.0 41.5 %layer.1 = bf16[128,512]{1,0:T(8,128)(2,1)} custom-call(bf16[128,640]{1,0:T(8,128)(2,1)} %refs_0_.1, s32[1,128]{1,0:T(1,128)} %bitcast.5, f32[1,5120]{1,0:T(1,128)} %bitcast.4, f32[1,128]{1,0:T(1,128)} %bitcast.6, f32[1,128]{1,0:T(1,128)} %bitcast.7, bf16[80,512]{1,0:T(8,128)(2,1)} %refs_5_.1, bf16[80,128]{1,0:T(8,128)(2,1)} %refs_6_.1, bf16[80,128]{1,0:T(8,128)(2,1)} %refs_7_.1), custom_call_target="tpu_custom_call" | custom-call | tf_op jit(solution)/shard_map/layer/pallas_call | solution.py:404
  41.5 1.6 %copy.10 = bf16[128,512]{1,0:T(8,128)(2,1)} copy(bf16[128,512]{1,0:T(8,128)(2,1)} %layer.1) | data formatting | bytes 262144

commit v3 on v2

--- a/solution.py
+++ b/solution.py
@@ -26,11 +26,11 @@
     (STEP, 2, 2, 1), (MEET, 3), (SEND, 3, False), (SEND, 1, False), (SEND, 2, False), (PASS, 0, False), (SQUARES,),
     (STEP, 0, 3, 0), (TABLES,), (STEP, 0, 3, 1), (PASS, 3, False), (STEP, 1, 3, 0), (STEP, 1, 3, 1),
     (PASS, 0, True), (PASS, 1, False), (STEP, 2, 3, 0), (STEP, 2, 3, 1), (PASS, 3, True), (PASS, 2, False),
-    (LAST, 0), (LAST, 1), (PASS, 1, True), (SEND, 0, False), (LAST, 2), (PASS, 2, True), (SUM,), (CORE, 3),
-    (SCALE,), (CORE, 0), (TURN, 3), (CORE, 1), (SEND, 0, True), (PROJECT, 0, 3), (TURN, 0), (PROJECT, 1, 3),
-    (CORE, 2), (TURN, 1), (PROJECT, 0, 1), (PROJECT, 1, 1), (PROJECT, 2, 3), (TURN, 2), (PROJECT, 0, 2),
-    (PROJECT, 1, 2), (PROJECT, 2, 1), (PROJECT, 2, 2), (PROJECT, 0, 0), (PROJECT, 1, 0), (PROJECT, 2, 0), (DONE, 0),
-    (DONE, 1), (DONE, 2),
+    (LAST, 0), (LAST, 1), (PASS, 1, True), (SEND, 0, False), (LAST, 2), (PASS, 2, True), (CORE, 3), (TURN, 3),
+    (CORE, 1), (SEND, 0, True), (PROJECT, 0, 3), (PROJECT, 1, 3), (CORE, 2), (TURN, 1), (PROJECT, 0, 1),
+    (PROJECT, 1, 1), (PROJECT, 2, 3), (TURN, 2), (PROJECT, 0, 2), (PROJECT, 1, 2), (PROJECT, 2, 1), (PROJECT, 2, 2),
+    (CORE, 0), (SUM,), (TURN, 0), (PROJECT, 0, 0), (PROJECT, 1, 0), (PROJECT, 2, 0), (SCALE,), (DONE, 0), (DONE, 1),
+    (DONE, 2),
 )
 ORDER_1 = (
     (PAIR, 0), (PAIR, 1), (PAIR, 2), (SWAP, 3), (SWAP, 1), (SWAP, 2), (STEP, 0, 1, 0), (STEP, 1, 1, 0),
@@ -39,11 +39,11 @@
     (SEND, 1, True), (SEND, 2, True), (STEP, 0, 2, 1), (MEET, 2), (SQUARES,), (STEP, 1, 2, 1), (PASS, 3, True),
     (STEP, 2, 2, 0), (STEP, 2, 2, 1), (PASS, 1, True), (TABLES,), (PASS, 0, False), (STEP, 0, 3, 0),
     (STEP, 0, 3, 1), (PASS, 3, False), (PASS, 2, True), (STEP, 1, 3, 0), (STEP, 1, 3, 1), (PASS, 1, False),
-    (SEND, 0, True), (STEP, 2, 3, 0), (STEP, 2, 3, 1), (PASS, 2, False), (LAST, 0), (SUM,), (LAST, 1), (SCALE,),
-    (LAST, 2), (CORE, 3), (TURN, 3), (CORE, 1), (PROJECT, 0, 3), (PROJECT, 1, 3), (PROJECT, 2, 3), (TURN, 1),
-    (CORE, 2), (PROJECT, 0, 1), (PROJECT, 1, 1), (PROJECT, 2, 1), (TURN, 2), (PASS, 0, True), (CORE, 0),
-    (PROJECT, 0, 2), (PROJECT, 1, 2), (PROJECT, 2, 2), (TURN, 0), (PROJECT, 0, 0), (PROJECT, 1, 0), (PROJECT, 2, 0),
-    (DONE, 0), (DONE, 1), (DONE, 2),
+    (SEND, 0, True), (STEP, 2, 3, 0), (STEP, 2, 3, 1), (PASS, 2, False), (LAST, 0), (LAST, 1), (LAST, 2), (CORE, 3),
+    (TURN, 3), (CORE, 1), (PROJECT, 0, 3), (PROJECT, 1, 3), (PROJECT, 2, 3), (TURN, 1), (CORE, 2), (PROJECT, 0, 1),
+    (PROJECT, 1, 1), (PROJECT, 2, 1), (TURN, 2), (PASS, 0, True), (PROJECT, 0, 2), (PROJECT, 1, 2), (PROJECT, 2, 2),
+    (CORE, 0), (SUM,), (TURN, 0), (PROJECT, 0, 0), (PROJECT, 1, 0), (PROJECT, 2, 0), (SCALE,), (DONE, 0), (DONE, 1),
+    (DONE, 2),
 )
 ORDER_2 = (
     (PAIR, 0), (SWAP, 3), (SWAP, 1), (SWAP, 2), (PAIR, 1), (STEP, 0, 1, 0), (PAIR, 2), (STEP, 1, 1, 0),
@@ -53,10 +53,9 @@
     (STEP, 2, 2, 0), (STEP, 2, 2, 1), (PASS, 1, True), (TABLES,), (PASS, 3, False), (STEP, 0, 3, 0),
     (SEND, 0, True), (STEP, 0, 3, 1), (PASS, 2, True), (PASS, 1, False), (STEP, 1, 3, 0), (STEP, 1, 3, 1),
     (PASS, 2, False), (STEP, 2, 3, 0), (CORE, 3), (STEP, 2, 3, 1), (CORE, 1), (LAST, 0), (TURN, 3), (CORE, 2),
-    (PASS, 0, True), (SUM,), (TURN, 1), (LAST, 1), (TURN, 2), (SCALE,), (LAST, 2), (PROJECT, 0, 3), (PROJECT, 0, 1),
-    (PROJECT, 0, 2), (PROJECT, 1, 3), (PROJECT, 1, 1), (PROJECT, 1, 2), (PROJECT, 2, 3), (PROJECT, 2, 1),
-    (PROJECT, 2, 2), (CORE, 0), (TURN, 0), (PROJECT, 0, 0), (PROJECT, 1, 0), (PROJECT, 2, 0), (DONE, 0), (DONE, 1),
-    (DONE, 2),
+    (PASS, 0, True), (TURN, 1), (LAST, 1), (TURN, 2), (LAST, 2), (PROJECT, 0, 3), (PROJECT, 0, 1), (PROJECT, 0, 2),
+    (PROJECT, 1, 3), (PROJECT, 1, 1), (PROJECT, 1, 2), (PROJECT, 2, 3), (PROJECT, 2, 1), (PROJECT, 2, 2), (CORE, 0),
+    (SUM,), (TURN, 0), (PROJECT, 0, 0), (PROJECT, 1, 0), (PROJECT, 2, 0), (SCALE,), (DONE, 0), (DONE, 1), (DONE, 2),
 )
 ORDER_3 = (
     (PAIR, 0), (SWAP, 3), (SWAP, 1), (SWAP, 2), (PAIR, 1), (SQUARES,), (PAIR, 2), (STEP, 0, 1, 0), (STEP, 1, 1, 0),
@@ -64,12 +63,11 @@
     (SEND, 1, True), (SEND, 1, False), (SEND, 2, True), (SEND, 2, False), (STEP, 1, 1, 1), (STEP, 2, 1, 1),
     (STEP, 0, 2, 0), (STEP, 1, 2, 0), (STEP, 0, 2, 1), (PASS, 3, False), (PASS, 3, True), (STEP, 1, 2, 1),
     (STEP, 2, 2, 0), (PASS, 1, False), (PASS, 1, True), (TABLES,), (STEP, 2, 2, 1), (STEP, 0, 3, 0),
-    (PASS, 2, False), (PASS, 2, True), (STEP, 0, 3, 1), (STEP, 1, 3, 0), (SUM,), (CORE, 3), (STEP, 1, 3, 1),
-    (CORE, 1), (STEP, 2, 3, 0), (SCALE,), (TURN, 3), (PASS, 0, True), (STEP, 2, 3, 1), (TURN, 1), (CORE, 2),
-    (LAST, 0), (PASS, 0, False), (LAST, 1), (TURN, 2), (CORE, 0), (LAST, 2), (PROJECT, 0, 3), (TURN, 0),
-    (PROJECT, 0, 1), (PROJECT, 0, 2), (PROJECT, 1, 3), (PROJECT, 1, 1), (PROJECT, 1, 2), (PROJECT, 2, 3),
-    (PROJECT, 2, 1), (PROJECT, 2, 2), (PROJECT, 0, 0), (PROJECT, 1, 0), (PROJECT, 2, 0), (DONE, 0), (DONE, 1),
-    (DONE, 2),
+    (PASS, 2, False), (PASS, 2, True), (STEP, 0, 3, 1), (STEP, 1, 3, 0), (CORE, 3), (STEP, 1, 3, 1), (CORE, 1),
+    (STEP, 2, 3, 0), (TURN, 3), (PASS, 0, True), (STEP, 2, 3, 1), (TURN, 1), (CORE, 2), (LAST, 0), (PASS, 0, False),
+    (LAST, 1), (TURN, 2), (LAST, 2), (PROJECT, 0, 3), (PROJECT, 0, 1), (PROJECT, 0, 2), (PROJECT, 1, 3),
+    (PROJECT, 1, 1), (PROJECT, 1, 2), (PROJECT, 2, 3), (PROJECT, 2, 1), (PROJECT, 2, 2), (CORE, 0), (SUM,),
+    (TURN, 0), (PROJECT, 0, 0), (PROJECT, 1, 0), (PROJECT, 2, 0), (SCALE,), (DONE, 0), (DONE, 1), (DONE, 2),
 )
 ORDERS = (ORDER_0, ORDER_1, ORDER_2, ORDER_3)
 LOCAL = D // (NH * NK)

time: 43.8 us -> 43.8 us (level)
  no operation moved by 1% of the time
where the time goes in v3:
time: 43.8 us; the launch traced here: 43 us
  Pallas kernels  41.5 us (95%)
  local copies, waits for them, and re-layouts  1.57 us (4%)
    pallas_call x1, Pallas kernels, per_device(): pl.pallas_call(kernel, name='layer', out_shape=jax.ShapeDtypeStruct((TOK,...  41.5 us
    unnamed x1, local copies, waits for them, and re-layouts  1.57 us

profile of v3, /device:TPU:1, one launch (start us, length us, event | category | flops | bytes accessed | tf_op | source)
XLA Modules:
  0.0 43.0 jit_solution(13845126476501704667)
XLA Ops:
  0.0 41.5 %layer.1 = bf16[128,512]{1,0:T(8,128)(2,1)} custom-call(bf16[128,640]{1,0:T(8,128)(2,1)} %refs_0_.1, s32[1,128]{1,0:T(1,128)} %bitcast.5, f32[1,5120]{1,0:T(1,128)} %bitcast.4, f32[1,128]{1,0:T(1,128)} %bitcast.6, f32[1,128]{1,0:T(1,128)} %bitcast.7, bf16[80,512]{1,0:T(8,128)(2,1)} %refs_5_.1, bf16[80,128]{1,0:T(8,128)(2,1)} %refs_6_.1, bf16[80,128]{1,0:T(8,128)(2,1)} %refs_7_.1), custom_call_target="tpu_custom_call" | custom-call | tf_op jit(solution)/shard_map/layer/pallas_call | solution.py:402
  41.5 1.6 %copy.10 = bf16[128,512]{1,0:T(8,128)(2,1)} copy(bf16[128,512]{1,0:T(8,128)(2,1)} %layer.1) | data formatting | bytes 262144
